TPU v7x, 32 devices: a whole 2x2x4 slice. The times are simulated.
32 devices in a mesh: parts: 2 (over y), dp: 2 (over x), tensor: 4 (over z), sub: 2 (over core).
Axes of the slice: x: 2, y: 2, z: 4, core: 2. Of those that a mesh axis runs over, the one named last changes fastest.
Arguments:
- acts: bfloat16 [512, 5120], P(('parts', 'tensor'), ('dp', 'sub')), parts along dimension 0, may hold values from -6 to 6
- frozen_weight: bfloat16 [5120, 25600], P(('dp', 'sub'), 'tensor'), may hold values from -0.078125 to 0.078125
- adapter_down_maps: bfloat16 [8, 5120, 64], P(('parts', 'tensor'), ('dp', 'sub')), parts along dimension 0, may hold values from -0.078125 to 0.078125
- adapter_up_maps: bfloat16 [8, 64, 25600], P(('parts', 'dp', 'sub'), None, 'tensor'), parts along dimension 0, may hold values from -0.75 to 0.75
- down_first_moment: float32 [8, 5120, 64], P(('parts', 'tensor'), ('dp', 'sub')), parts along dimension 0, may hold values from -0.75 to 0.75
- down_second_moment: float32 [8, 5120, 64], P(('parts', 'tensor'), ('dp', 'sub')), parts along dimension 0, may hold values from 0.0001 to 0.01
- up_first_moment: float32 [8, 64, 25600], P(('parts', 'dp', 'sub'), None, 'tensor'), parts along dimension 0, may hold values from -0.078125 to 0.078125
- up_second_moment: float32 [8, 64, 25600], P(('parts', 'dp', 'sub'), None, 'tensor'), parts along dimension 0, may hold values from 1e-06 to 0.0001
- readout: bfloat16 [512, 25600], P(('parts', 'dp', 'sub'), 'tensor'), parts along dimension 0, may hold values from -0.0390625 to 0.0390625
- adapter_index_rows: int32 [512, 1], P('parts'), parts along dimension 0, may hold values from 0 to 3; in each aligned block of 64 rows (0 to 63, 64 to 127, ...) at most 32 rows name the same one
- preference_pair_rows: int32 [256, 2], P(('parts', 'dp', 'sub')), parts along dimension 0, may hold values from 0 to 63, as said below
Outputs:
- updated_down_maps: bfloat16 [8, 5120, 64], P(('parts', 'tensor'), ('dp', 'sub')), parts along dimension 0
- updated_down_first: float32 [8, 5120, 64], P(('parts', 'tensor'), ('dp', 'sub')), parts along dimension 0
- updated_down_second: float32 [8, 5120, 64], P(('parts', 'tensor'), ('dp', 'sub')), parts along dimension 0
- updated_up_maps: bfloat16 [8, 64, 25600], P(('parts', 'dp', 'sub'), None, 'tensor'), parts along dimension 0
- updated_up_first: float32 [8, 64, 25600], P(('parts', 'dp', 'sub'), None, 'tensor'), parts along dimension 0
- updated_up_second: float32 [8, 64, 25600], P(('parts', 'dp', 'sub'), None, 'tensor'), parts along dimension 0
There are 2 independent parts, one for each index of `parts`. A program takes and returns all parts, laid end to end along the dimension named above; an argument that names none is the same for every part. Nothing has to cross between parts.
Inputs may be any that keep to these rules, and one draw needn't show every extreme that they name: `adapter_index_rows`: within the rows of one group (aligned blocks of 64 rows) no adapter is named by more than 32 rows, and in every draw some group has an adapter named by exactly 32 rows. `preference_pair_rows`: the pairs of group q are rows q * (32) to (q + 1) * 32 - 1; together their two columns name every row index of the group exactly once.
All inputs are finite; a program needn't handle non-finite values.
Results may differ from a plain program's by a relative error of at most 0.0034.
Values may be sent and summed in bfloat16 or wider, within the bound.
A program may use at most 128 MiB of HBM per device.

v0:
```python
import jax
import jax.numpy as jnp
from jax import lax
from jax.sharding import PartitionSpec as P

adapter_scale = 2.0
beta_pref = 0.1
learn_rate = 0.001
first_decay = 0.9
second_decay = 0.95
first_fix = 1.0 - 2.656139888758747e-05
second_fix = 1.0 - 0.005920529220334
adam_eps = 1e-08


def swish_slope(pre_act):
    sigmoid_of = jax.nn.sigmoid(pre_act)
    return sigmoid_of * (1.0 + pre_act * (1.0 - sigmoid_of))


def moment_update_step(param, mean_old, square_old, grad):
    new_mean = first_decay * mean_old + (1.0 - first_decay) * grad
    new_square = second_decay * square_old + (1.0 - second_decay) * grad * grad
    update_step = new_mean / first_fix / (jnp.sqrt(new_square / second_fix) + adam_eps)
    new_param = (param.astype(jnp.float32) - learn_rate * update_step).astype(jnp.bfloat16)
    return (new_param, new_mean, new_square)


def body(
    acts,
    frozen_weight,
    adapter_down_maps,
    adapter_up_maps,
    down_first_moment,
    down_second_moment,
    up_first_moment,
    up_second_moment,
    readout,
    adapter_index_rows,
    preference_pair_rows,
):
    group_count = lax.axis_size(("dp", "sub"))
    group_index = lax.axis_index(("dp", "sub"))
    tensor_index = lax.axis_index("tensor")
    reduced_rank_output = adapter_down_maps.shape[2]
    local_down_maps = adapter_down_maps.shape[0]
    local_up_maps = adapter_up_maps.shape[0]
    adapters = local_up_maps * group_count
    group_rows = readout.shape[0]
    columns = readout.shape[1]
    ids_all = adapter_index_rows[:, 0]
    catalog = jnp.arange(adapters, dtype=jnp.int32)
    member_all = (ids_all[:, None] == catalog[None, :]).astype(jnp.float32)
    member_mine = lax.dynamic_slice_in_dim(
        member_all, tensor_index * local_down_maps, local_down_maps, 1
    )
    rows_all = lax.all_gather(acts, "tensor", axis=0, tiled=True)
    base_part = jnp.dot(rows_all, frozen_weight, preferred_element_type=jnp.float32)
    down_maps_total = lax.all_gather(adapter_down_maps, "tensor", axis=0, tiled=True)
    products = jnp.einsum(
        "rd,adk->rak", rows_all, down_maps_total, preferred_element_type=jnp.float32
    )
    shrink_part = jnp.sum(products * member_all[:, :, None], axis=1)
    base_terms = base_part.astype(jnp.bfloat16).reshape(group_count, group_rows, columns)
    shrink_terms = shrink_part.astype(jnp.bfloat16).reshape(
        group_count, group_rows, reduced_rank_output
    )
    base_arrived, shrink_arrived = (
        lax.all_to_all(base_terms, ("dp", "sub"), split_axis=0, concat_axis=0, tiled=True),
        lax.all_to_all(shrink_terms, ("dp", "sub"), split_axis=0, concat_axis=0, tiled=True),
    )
    frozen_sum = jnp.sum(base_arrived.astype(jnp.float32), axis=0)
    shrink = jnp.sum(shrink_arrived.astype(jnp.float32), axis=0)
    shrink_low = shrink.astype(jnp.bfloat16)
    my_ids = lax.dynamic_slice_in_dim(ids_all, group_index * group_rows, group_rows, 0)
    capacity = 2 * group_rows // adapters
    member_int = (my_ids[:, None] == catalog[None, :]).astype(jnp.int32)
    before = jnp.cumsum(member_int, axis=0) - member_int
    slot_index = jnp.sum(before * member_int, axis=1)
    position = my_ids * capacity + slot_index
    placing = (
        position[None, :] == jnp.arange(adapters * capacity, dtype=jnp.int32)[:, None]
    ).astype(jnp.bfloat16)
    outgoing = (
        jnp.dot(placing, shrink_low, preferred_element_type=jnp.float32)
        .astype(jnp.bfloat16)
        .reshape(adapters, capacity, reduced_rank_output)
    )
    received = lax.all_to_all(outgoing, ("dp", "sub"), split_axis=0, concat_axis=0, tiled=True)
    slot_count = received.shape[1]
    grid_rank = received.reshape(group_count, local_up_maps, slot_count, reduced_rank_output)
    expanded = jnp.einsum(
        "gjcr,jrf->gjcf", grid_rank, adapter_up_maps, preferred_element_type=jnp.float32
    ).astype(jnp.bfloat16)
    returned = lax.all_to_all(
        expanded.reshape(group_count * local_up_maps, slot_count, columns),
        ("dp", "sub"),
        split_axis=0,
        concat_axis=0,
        tiled=True,
    )
    returned, arrived = (returned, received)
    widen_rows = jnp.dot(
        placing.T,
        returned.reshape(adapters * capacity, columns),
        preferred_element_type=jnp.float32,
    ).astype(jnp.bfloat16)
    policy_scores = frozen_sum + adapter_scale * widen_rows.astype(jnp.float32)
    read_float = readout.astype(jnp.float32)
    score_policy, score_base = lax.psum(
        (
            jnp.sum(read_float * jax.nn.silu(policy_scores), axis=1),
            jnp.sum(read_float * jax.nn.silu(frozen_sum), axis=1),
        ),
        "tensor",
    )
    margin_rows = score_policy - score_base
    row_number = jnp.arange(group_rows, dtype=jnp.int32)
    pick_chosen = (preference_pair_rows[:, 0:1] == row_number[None, :]).astype(jnp.float32)
    pick_rejected = (preference_pair_rows[:, 1:2] == row_number[None, :]).astype(jnp.float32)
    margin = beta_pref * (
        jnp.sum(pick_chosen * margin_rows[None, :], axis=1)
        - jnp.sum(pick_rejected * margin_rows[None, :], axis=1)
    )
    weight = beta_pref * jax.nn.sigmoid(-margin)
    row_grad = jnp.sum((pick_rejected - pick_chosen) * weight[:, None], axis=0)
    output_gradient = (row_grad[:, None] * read_float * swish_slope(policy_scores)).astype(
        jnp.bfloat16
    )
    outgoing_grad = (
        jnp.dot(placing, output_gradient, preferred_element_type=jnp.float32)
        .astype(jnp.bfloat16)
        .reshape(adapters, capacity, columns)
    )
    arrived_grad = lax.all_to_all(
        outgoing_grad, ("dp", "sub"), split_axis=0, concat_axis=0, tiled=True
    )
    grid_rank = arrived.reshape(group_count, local_up_maps, capacity, reduced_rank_output)
    grid_grad = arrived_grad.reshape(group_count, local_up_maps, capacity, columns)
    up_gradient = adapter_scale * jnp.einsum(
        "gjcr,gjcf->jrf", grid_rank, grid_grad, preferred_element_type=jnp.float32
    )
    rank_slots = jnp.einsum(
        "gjcf,jrf->gjcr", grid_grad, adapter_up_maps, preferred_element_type=jnp.float32
    )
    rank_back = lax.all_to_all(
        rank_slots.reshape(group_count * local_up_maps, capacity, reduced_rank_output).astype(
            jnp.bfloat16
        ),
        ("dp", "sub"),
        split_axis=0,
        concat_axis=0,
        tiled=True,
    ).astype(jnp.float32)
    rank_portion = jnp.dot(
        placing.astype(jnp.float32).T,
        rank_back.reshape(adapters * capacity, reduced_rank_output),
        precision=lax.Precision.HIGHEST,
    )
    rank_gradient = (adapter_scale * lax.psum(rank_portion, "tensor")).astype(jnp.bfloat16)
    rank_all = lax.all_gather(rank_gradient, ("dp", "sub"), axis=0, tiled=True)
    spread_back = (member_mine[:, :, None] * rank_all.astype(jnp.float32)[:, None, :]).astype(
        jnp.bfloat16
    )
    down_gradient = jnp.einsum(
        "rd,rjk->jdk", rows_all, spread_back, preferred_element_type=jnp.float32
    )
    updated_down_maps, updated_down_first, updated_down_second = moment_update_step(
        adapter_down_maps, down_first_moment, down_second_moment, down_gradient
    )
    updated_up_maps, updated_up_first, updated_up_second = moment_update_step(
        adapter_up_maps, up_first_moment, up_second_moment, up_gradient
    )
    return (
        updated_down_maps,
        updated_down_first,
        updated_down_second,
        updated_up_maps,
        updated_up_first,
        updated_up_second,
    )


def solution(mesh):
    placed = (
        P(("parts", "tensor"), ("dp", "sub")),
        P(("dp", "sub"), "tensor"),
        P(("parts", "tensor"), ("dp", "sub"), None),
        P(("parts", "dp", "sub"), None, "tensor"),
        P(("parts", "tensor"), ("dp", "sub"), None),
        P(("parts", "tensor"), ("dp", "sub"), None),
        P(("parts", "dp", "sub"), None, "tensor"),
        P(("parts", "dp", "sub"), None, "tensor"),
        P(("parts", "dp", "sub"), "tensor"),
        P("parts", None),
        P(("parts", "dp", "sub"), None),
    )
    return jax.shard_map(
        body,
        mesh=mesh,
        in_specs=placed,
        out_specs=(
            P(("parts", "tensor"), ("dp", "sub"), None),
            P(("parts", "tensor"), ("dp", "sub"), None),
            P(("parts", "tensor"), ("dp", "sub"), None),
            P(("parts", "dp", "sub"), None, "tensor"),
            P(("parts", "dp", "sub"), None, "tensor"),
            P(("parts", "dp", "sub"), None, "tensor"),
        ),
        check_vma=False,
    )
```

profile of v0, /device:TPU:0, one launch (start us, length us, event | category | flops | bytes accessed | tf_op | source)
XLA Modules:
  0.0 203.8 jit_solution(13545153758072854754)
XLA Ops:
  0.6 19.8 %all_gather.9 = bf16[256,1280]{1,0:T(8,128)(2,1)S(1)} all-gather(bf16[64,1280]{1,0:T(8,128)(2,1)} %param.11), channel_id=1, replica_groups=mesh['parts'=2,'dp'=2,'tensor'=4,'sub'=2] {'tensor'}, dimensions={0}, use_global_device_ids=true | all-gather | bytes 819200 | tf_op jit(solution)/shard_map/all_gather | solution.py:57
  20.5 16.3 %all_gather.10 = bf16[4,1280,64]{1,2,0:T(8,128)(2,1)S(1)} all-gather(bf16[1,1280,64]{1,2,0:T(8,128)(2,1)} %param.13), channel_id=1, replica_groups=mesh['parts'=2,'dp'=2,'tensor'=4,'sub'=2] {'tensor'}, dimensions={0}, use_global_device_ids=true | all-gather | bytes 819200 | tf_op jit(solution)/shard_map/all_gather | solution.py:59
  36.8 0.4 fusion.21
  37.2 0.1 convert_element_type.92
  37.3 0.7 reshape.118
  38.1 3.3 %all-to-all-start.1 = ((bf16[4,2,2048]{2,1,0:T(2,128)(2,1)}), bf16[4,2,2048]{2,1,0:T(2,128)(2,1)S(1)}, u32[]{:S(2)}, u32[]{:S(2)}) async-start(bf16[4,2,2048]{2,1,0:T(2,128)(2,1)} %reshape.118), calls=%async_computation.1 | async-start | bytes 65536 | tf_op jit(solution)/shard_map/all_to_all | solution.py:70
  41.4 0.1 dynamic-slice_bitcast_fusion
  41.4 0.1 fusion.17
  41.5 0.1 reduce_window_sum.11
  41.6 0.2 select_reduce_fusion
  41.8 0.1 multiply_add_fusion.1
  41.9 3.4 %all-to-all-done.1 = bf16[4,2,2048]{2,1,0:T(2,128)(2,1)S(1)} async-done(((bf16[4,2,2048]{2,1,0:T(2,128)(2,1)}), bf16[4,2,2048]{2,1,0:T(2,128)(2,1)S(1)}, u32[]{:S(2)}, u32[]{:S(2)}) %all-to-all-start.1) | async-done | bytes 32800 | tf_op jit(solution)/shard_map/all_to_all | solution.py:70
  45.3 0.1 reshape.119
  45.4 0.1 convolution_convert_fusion.5
  45.5 0.1 copy.25
  45.7 0.7 reshape.120
  46.4 3.3 %all-to-all-start.2 = ((bf16[4,2,1024]{2,1,0:T(2,128)(2,1)}), bf16[4,2,1024]{2,1,0:T(2,128)(2,1)S(1)}, u32[]{:S(2)}, u32[]{:S(2)}) async-start(bf16[4,2,1024]{2,1,0:T(2,128)(2,1)} %reshape.120), calls=%async_computation.2 | async-start | bytes 32768 | tf_op jit(solution)/shard_map/all_to_all | solution.py:89
  49.7 0.0 copy-done.1
  49.7 11.5 %convolution_convert_fusion = bf16[256,6400]{1,0:T(8,128)(2,1)} fusion(bf16[256,1280]{1,0:T(8,128)(2,1)S(1)} %all_gather.9, bf16[1280,6400]{1,0:T(8,128)(2,1)} %param.12), kind=kOutput, calls=%fused_computation | convolution fusion | flops 4195942400 | bytes 20316160 | tf_op jit(solution)/shard_map/dot_general | solution.py:58
  61.2 0.0 all-to-all-done.2
  61.2 3.7 %all-to-all-start = ((bf16[4,64,6400]{2,1,0:T(8,128)(2,1)}), bf16[4,64,6400]{2,1,0:T(8,128)(2,1)S(1)}, u32[]{:S(2)}, u32[]{:S(2)}) async-start(bf16[4,64,6400]{2,1,0:T(8,128)(2,1)} %bitcast.56), calls=%async_computation | async-start | bytes 6553600 | tf_op jit(solution)/shard_map/all_to_all | solution.py:69
  64.9 0.1 reshape.121
  65.0 2.9 %convolution_convert_fusion.2 = bf16[4,32,6400]{2,1,0:T(8,128)(2,1)} fusion(bf16[4,32,64]{2,1,0:T(8,128)(2,1)S(1)} %reshape.121, bf16[1,64,6400]{2,1,0:T(8,128)(2,1)} %param.14), kind=kOutput, calls=%fused_computation.2 | convolution fusion | flops 105676800 | bytes 2473984 | tf_op jit(solution)/shard_map/gjcr,jrf->gjcf/dot_general | solution.py:92
  67.9 35.3 %all-to-all-done = bf16[4,64,6400]{2,1,0:T(8,128)(2,1)S(1)} async-done(((bf16[4,64,6400]{2,1,0:T(8,128)(2,1)}), bf16[4,64,6400]{2,1,0:T(8,128)(2,1)S(1)}, u32[]{:S(2)}, u32[]{:S(2)}) %all-to-all-start) | async-done | bytes 3276832 | tf_op jit(solution)/shard_map/all_to_all | solution.py:69
  103.2 4.3 %all-to-all-start.3 = ((bf16[4,32,6400]{2,1,0:T(8,128)(2,1)}), bf16[4,32,6400]{2,1,0:T(8,128)(2,1)}, u32[]{:S(2)}, u32[]{:S(2)}) async-start(bf16[4,32,6400]{2,1,0:T(8,128)(2,1)} %convolution_convert_fusion.2), calls=%async_computation.3 | async-start | bytes 3276800 | tf_op jit(solution)/shard_map/all_to_all | solution.py:95
  107.6 0.0 copy-done.5
  107.6 1.6 convert_reduce_fusion
  109.2 19.2 %all-to-all-done.3 = bf16[4,32,6400]{2,1,0:T(8,128)(2,1)} async-done(((bf16[4,32,6400]{2,1,0:T(8,128)(2,1)}), bf16[4,32,6400]{2,1,0:T(8,128)(2,1)}, u32[]{:S(2)}, u32[]{:S(2)}) %all-to-all-start.3) | async-done | bytes 1638432 | tf_op jit(solution)/shard_map/all_to_all | solution.py:95
  128.4 3.5 %fusion.4 = (f32[64]{0:T(128)S(1)}, f32[64]{0:T(128)S(1)}, f32[64,6400]{1,0:T(8,128)S(1)}) fusion(bf16[64,6400]{1,0:T(8,128)(2,1)} %param.19, f32[64,6400]{1,0:T(8,128)} %convert_reduce_fusion, bf16[128,6400]{1,0:T(8,128)(2,1)} %bitcast.12, s32[64]{0:T(128)S(1)} %multiply_add_fusion.1), kind=kOutput, calls=%fused_computation.14 | convolution fusion | flops 111828864 | bytes 5735168 | tf_op jit(solution)/shard_map/dot_general | solution.py:103
  132.0 11.0 %all-reduce = (f32[64]{0:T(128)S(1)}, f32[64]{0:T(128)S(1)}) all-reduce(f32[64]{0:T(128)S(1)} %get-tuple-element.7, f32[64]{0:T(128)S(1)} %get-tuple-element.6), channel_id=1, replica_groups=mesh['parts'=2,'dp'=2,'tensor'=4,'sub'=2] {'tensor'}, use_global_device_ids=true, to_apply=%region_6.7 | all-reduce | flops 128 | bytes 1024 | tf_op jit(solution)/shard_map/psum | solution.py:110
  143.0 0.2 select_reduce_fusion.1
  143.2 0.1 multiply_reduce_fusion.1
  143.3 2.2 %convolution_convert_fusion.1 = bf16[128,6400]{1,0:T(8,128)(2,1)} fusion(bf16[64,6400]{1,0:T(8,128)(2,1)S(1)} %copy-done.6, f32[64,6400]{1,0:T(8,128)S(1)} %get-tuple-element.20, f32[64]{0:T(128)S(1)} %multiply_reduce_fusion.1, s32[64]{0:T(128)S(1)} %multiply_add_fusion.1), kind=kOutput, calls=%fused_computation.1 | convolution fusion | flops 110190592 | bytes 4096512 | tf_op jit(solution)/shard_map/dot_general | solution.py:131
  145.5 3.7 %all-to-all-start.4 = ((bf16[4,32,6400]{2,1,0:T(8,128)(2,1)}), bf16[4,32,6400]{2,1,0:T(8,128)(2,1)S(1)}, u32[]{:S(2)}, u32[]{:S(2)}) async-start(bf16[4,32,6400]{2,1,0:T(8,128)(2,1)} %bitcast.58), calls=%async_computation.4 | async-start | bytes 3276800 | tf_op jit(solution)/shard_map/all_to_all | solution.py:135
  149.3 20.7 %all-to-all-done.4 = bf16[4,32,6400]{2,1,0:T(8,128)(2,1)S(1)} async-done(((bf16[4,32,6400]{2,1,0:T(8,128)(2,1)}), bf16[4,32,6400]{2,1,0:T(8,128)(2,1)S(1)}, u32[]{:S(2)}, u32[]{:S(2)}) %all-to-all-start.4) | async-done | bytes 1638432 | tf_op jit(solution)/shard_map/all_to_all | solution.py:135
  170.0 0.0 copy-done
  170.0 0.6 convolution_convert_fusion.4
  170.6 0.7 reshape.122
  171.3 3.3 %all-to-all-start.5 = ((bf16[4,2,1024]{2,1,0:T(2,128)(2,1)}), bf16[4,2,1024]{2,1,0:T(2,128)(2,1)S(1)}, u32[]{:S(2)}, u32[]{:S(2)}) async-start(bf16[4,2,1024]{2,1,0:T(2,128)(2,1)} %reshape.122), calls=%async_computation.5 | async-start | bytes 32768 | tf_op jit(solution)/shard_map/all_to_all | solution.py:146
  174.5 0.0 copy-start.3
  174.6 5.5 %subtract_convert_fusion = (bf16[1,64,6400]{2,1,0:T(8,128)(2,1)}, f32[1,64,6400]{2,1,0:T(8,128)}, f32[1,64,6400]{2,1,0:T(8,128)}) fusion(bf16[1,64,6400]{2,1,0:T(8,128)(2,1)S(1)} %copy-done, f32[1,64,6400]{2,1,0:T(8,128)} %param.17, f32[1,64,6400]{2,1,0:T(8,128)} %param.18, bf16[4,32,64]{2,1,0:T(8,128)(2,1)S(1)} %reshape.121, ...), kind=kOutput, calls=%fused_computation.19 | convolution fusion | flops 111411200 | bytes 9846784 | tf_op jit(solution)/shard_map/gjcr,gjcf->jrf/dot_general | solution.py:140
  180.0 0.0 all-to-all-done.5
  180.0 0.1 reshape.123
  180.1 0.2 fusion.11
  180.3 15.8 %psum.23 = f32[64,64]{1,0:T(8,128)S(1)} all-reduce(f32[64,64]{1,0:T(8,128)S(1)} %fusion.11), channel_id=1, replica_groups=mesh['parts'=2,'dp'=2,'tensor'=4,'sub'=2] {'tensor'}, use_global_device_ids=true, to_apply=%region_12.13 | all-reduce | flops 4096 | bytes 32768 | tf_op jit(solution)/shard_map/psum | solution.py:160
  196.1 5.2 %all_gather.11 = bf16[256,64]{1,0:T(8,128)(2,1)S(1)} all-gather(bf16[64,64]{1,0:T(8,128)(2,1)S(1)} %multiply_convert_fusion.2), channel_id=1, replica_groups=mesh['parts'=2,'dp'=2,'tensor'=4,'sub'=2] {'dp','sub'}, dimensions={0}, use_global_device_ids=true | all-gather | bytes 40960 | tf_op jit(solution)/shard_map/all_gather | solution.py:161
  201.4 0.0 copy-done.2
  201.4 2.5 %subtract_convert_fusion.1 = (bf16[1,1280,64]{1,2,0:T(8,128)(2,1)}, f32[1,1280,64]{1,2,0:T(8,128)}, f32[1,1280,64]{1,2,0:T(8,128)}) fusion(bf16[1,1280,64]{1,2,0:T(8,128)(2,1)S(1)} %copy-done.3, f32[1,1280,64]{1,2,0:T(8,128)} %param.15, f32[1,1280,64]{1,2,0:T(8,128)} %param.16, bf16[256,1280]{1,0:T(8,128)(2,1)S(1)} %copy-done.2, ...), kind=kOutput, calls=%fused_computation.27 | convolution fusion | flops 43220992 | bytes 2327552 | tf_op jit(solution)/shard_map/rd,rjk->jdk/dot_general | solution.py:165
  (18 shorter events, 0.1 us)
Async XLA Ops:
  0.6 36.2 %copy-start.4 = (s32[256,1]{0,1:T(1,128)S(1)}, s32[256,1]{0,1:T(1,128)}, u32[]{:S(2)}) copy-start(s32[256,1]{0,1:T(1,128)} %param.20) | copy-start | bytes 3076
  20.5 29.2 %copy-start.1 = (bf16[256,1280]{1,0:T(8,128)(2,1)}, bf16[256,1280]{1,0:T(8,128)(2,1)S(1)}, u32[]{:S(2)}) copy-start(bf16[256,1280]{1,0:T(8,128)(2,1)S(1)} %all_gather.9) | copy-start | bytes 1966084
  38.1 7.2 %all-to-all-start.1 = ((bf16[4,2,2048]{2,1,0:T(2,128)(2,1)}), bf16[4,2,2048]{2,1,0:T(2,128)(2,1)S(1)}, u32[]{:S(2)}, u32[]{:S(2)}) async-start(bf16[4,2,2048]{2,1,0:T(2,128)(2,1)} %reshape.118), calls=%async_computation.1 | async-start | bytes 65536 | tf_op jit(solution)/shard_map/all_to_all | solution.py:70
  46.4 14.8 %all-to-all-start.2 = ((bf16[4,2,1024]{2,1,0:T(2,128)(2,1)}), bf16[4,2,1024]{2,1,0:T(2,128)(2,1)S(1)}, u32[]{:S(2)}, u32[]{:S(2)}) async-start(bf16[4,2,1024]{2,1,0:T(2,128)(2,1)} %reshape.120), calls=%async_computation.2 | async-start | bytes 32768 | tf_op jit(solution)/shard_map/all_to_all | solution.py:89
  61.2 42.0 %all-to-all-start = ((bf16[4,64,6400]{2,1,0:T(8,128)(2,1)}), bf16[4,64,6400]{2,1,0:T(8,128)(2,1)S(1)}, u32[]{:S(2)}, u32[]{:S(2)}) async-start(bf16[4,64,6400]{2,1,0:T(8,128)(2,1)} %bitcast.56), calls=%async_computation | async-start | bytes 6553600 | tf_op jit(solution)/shard_map/all_to_all | solution.py:69
  67.9 39.7 %copy-start.5 = (s32[32,2]{0,1:T(2,128)S(1)}, s32[32,2]{0,1:T(2,128)}, u32[]{:S(2)}) copy-start(s32[32,2]{0,1:T(2,128)} %param.21) | copy-start | bytes 772
  103.2 25.2 %all-to-all-start.3 = ((bf16[4,32,6400]{2,1,0:T(8,128)(2,1)}), bf16[4,32,6400]{2,1,0:T(8,128)(2,1)}, u32[]{:S(2)}, u32[]{:S(2)}) async-start(bf16[4,32,6400]{2,1,0:T(8,128)(2,1)} %convolution_convert_fusion.2), calls=%async_computation.3 | async-start | bytes 3276800 | tf_op jit(solution)/shard_map/all_to_all | solution.py:95
  128.4 14.9 %copy-start.6 = (bf16[64,6400]{1,0:T(8,128)(2,1)S(1)}, bf16[64,6400]{1,0:T(8,128)(2,1)}, u32[]{:S(2)}) copy-start(bf16[64,6400]{1,0:T(8,128)(2,1)} %param.19) | copy-start | bytes 2457604
  145.5 24.5 %copy-start = (bf16[1,64,6400]{2,1,0:T(8,128)(2,1)S(1)}, bf16[1,64,6400]{2,1,0:T(8,128)(2,1)}, u32[]{:S(2)}) copy-start(bf16[1,64,6400]{2,1,0:T(8,128)(2,1)} %param.14) | copy-start | bytes 2457604
  145.5 24.5 %all-to-all-start.4 = ((bf16[4,32,6400]{2,1,0:T(8,128)(2,1)}), bf16[4,32,6400]{2,1,0:T(8,128)(2,1)S(1)}, u32[]{:S(2)}, u32[]{:S(2)}) async-start(bf16[4,32,6400]{2,1,0:T(8,128)(2,1)} %bitcast.58), calls=%async_computation.4 | async-start | bytes 3276800 | tf_op jit(solution)/shard_map/all_to_all | solution.py:135
  171.3 8.8 %all-to-all-start.5 = ((bf16[4,2,1024]{2,1,0:T(2,128)(2,1)}), bf16[4,2,1024]{2,1,0:T(2,128)(2,1)S(1)}, u32[]{:S(2)}, u32[]{:S(2)}) async-start(bf16[4,2,1024]{2,1,0:T(2,128)(2,1)} %reshape.122), calls=%async_computation.5 | async-start | bytes 32768 | tf_op jit(solution)/shard_map/all_to_all | solution.py:146
  174.5 26.8 %copy-start.2 = (bf16[256,1280]{1,0:T(8,128)(2,1)S(1)}, bf16[256,1280]{1,0:T(8,128)(2,1)}, u32[]{:S(2)}) copy-start(bf16[256,1280]{1,0:T(8,128)(2,1)} %copy-done.1) | copy-start | bytes 1966084
  174.5 26.8 %copy-start.3 = (bf16[1,1280,64]{1,2,0:T(8,128)(2,1)S(1)}, bf16[1,1280,64]{1,2,0:T(8,128)(2,1)}, u32[]{:S(2)}) copy-start(bf16[1,1280,64]{1,2,0:T(8,128)(2,1)} %param.13) | copy-start | bytes 491524
where the time goes:
time: 205 us; the launch traced here: 204 us
  waiting for transfers between devices  78.6 us (38%)
  blocking collectives  68.2 us (33%)
  matrix products  29.4 us (14%)
  starting transfers between devices  21.5 us (10%)
  local copies, waits for them, and re-layouts  2.82 us (1%)
  other arithmetic  2.43 us (1%)
    all_to_all x1, waiting for transfers between devices, body(): lax.all_to_all(base_terms, ('dp', 'sub'), split_axis=0, concat_axis=0, ti...  35.3 us
    all_to_all x1, waiting for transfers between devices, body(): lax.all_to_all(outgoing_grad, ('dp', 'sub'), split_axis=0, concat_axis=0,...  20.7 us
    all_gather x1, blocking collectives, body(): rows_all = lax.all_gather(acts, 'tensor', axis=0, tiled=True)  19.8 us
    all_to_all x1, waiting for transfers between devices, body(): lax.all_to_all(expanded.reshape(group_count * local_up_maps, slot_count,...  19.2 us
    all_gather x1, blocking collectives, body(): lax.all_gather(adapter_down_maps, 'tensor', axis=0, tiled=True)  16.3 us
    psum x1, blocking collectives, body(): lax.psum(rank_portion, 'tensor')  15.8 us
    dot_general x1, matrix products, body(): jnp.dot(rows_all, frozen_weight, preferred_element_type=jnp.float32)  11.5 us
    psum x1, blocking collectives, body(): lax.psum((jnp.sum(read_float * jax.nn.silu(policy_scores), axis=1), jnp.s...  11 us
  transfers between devices with their start and end apart: 6, of which 4 were waited for; matrix products, arithmetic and copies ran while one was open for 11% of the time, Pallas kernels for 0%

commit v1 on v0

--- a/solution.py
+++ b/solution.py
@@ -1,6 +1,10 @@
+import functools
+
 import jax
 import jax.numpy as jnp
 from jax import lax
+from jax.experimental import pallas as pl
+from jax.experimental.pallas import tpu as pltpu
 from jax.sharding import PartitionSpec as P
 
 adapter_scale = 2.0
@@ -181,6 +185,592 @@
     )
 
 
+def to_device(dp, t, s):
+    return {"dp": dp, "tensor": t, "sub": s}
+
+
+def remote(src, dst, send_sem, recv_sem, device):
+    return pltpu.make_async_remote_copy(
+        src_ref=src,
+        dst_ref=dst,
+        send_sem=send_sem,
+        recv_sem=recv_sem,
+        device_id=device,
+        device_id_type=pl.DeviceIdType.MESH,
+    )
+
+
+def rows_at(start, size):
+    return pl.ds(pl.multiple_of(start, size), size)
+
+
+def step_kernel(
+    T, chunk, acts, w, down, up, readout, ids, pairs,
+    upg, rank_out, acts_out,
+    acts_all, wbuf, own, sib_out, sib_in, x_out, x_in, upbuf, rd,
+    terms, terms_in, shrink_own, shrink_half, scat, pick,
+    margin_own, margin_in, grad_out, ug_own, ug_out, ug_in, gx_out, gx_in, gown,
+    rank_part, rank_in, rank_own, rank_all, rank_acc, score_acc,
+    acts_ss, acts_rs, w_sem, local_sem, sib_ss, sib_rs, x_ss, x_rs,
+    mat_ss, mat_rs, terms_ss, terms_rs, shrink_ss, shrink_rs, margin_ss, margin_rs,
+    ug_ss, ug_rs, gx_ss, gx_rs, out_sem, rank_ss, rank_rs, all_ss, all_rs,
+):
+    dp, t, s = lax.axis_index("dp"), lax.axis_index("tensor"), lax.axis_index("sub")
+    rows = acts_all.shape[0]
+    half = rows // 2
+    group = half // 2
+    columns = w.shape[1]
+    span = columns // 2
+    chunks = span // chunk
+    rank = down.shape[1]
+    share = half // (2 * T)
+    M = 2 * T
+    mine = dp * T + t
+    me = mine * 2 + s
+    sibling = to_device(dp, t, 1 - s)
+    across = to_device(1 - dp, t, s)
+    here = pl.multiple_of(dp * span, 128)
+    there = pl.multiple_of((1 - dp) * span, 128)
+
+    def w_copy(c):
+        base = jnp.where(c < chunks, 1 - dp, dp) * span
+        off = base + lax.rem(c, chunks) * chunk
+        return pltpu.make_async_copy(
+            w.at[:, pl.ds(pl.multiple_of(off, 128), chunk)], wbuf.at[c], w_sem.at[c]
+        )
+
+    def device_at(k):
+        number = lax.rem(me + k, 2 * M)
+        return number, number // (2 * T), lax.rem(number // 2, T), lax.rem(number, 2)
+
+    @pl.loop(0, 2)
+    def _(c):
+        w_copy(c).start()
+
+    up_local = pltpu.make_async_copy(up.at[:, pl.ds(here, span)], upbuf.at[0:group], local_sem.at[0])
+    rd_local = pltpu.make_async_copy(
+        readout.at[:, pl.ds(here, span)], rd.at[rows_at(dp * group, group)], local_sem.at[1]
+    )
+    own_slot = rows_at((lax.rem(t + s, 2) * 2 + t // 2) * group, group)
+    acts_local = pltpu.make_async_copy(acts, acts_all.at[own_slot], local_sem.at[2])
+    up_local.start()
+    rd_local.start()
+    acts_local.start()
+
+    barrier = pltpu.get_barrier_semaphore()
+
+    @pl.loop(1, 2 * M)
+    def _(k):
+        _, d, z, c = device_at(k)
+        pl.semaphore_signal(
+            barrier, inc=1, device_id=to_device(d, z, c), device_id_type=pl.DeviceIdType.MESH
+        )
+
+    pl.semaphore_wait(barrier, 2 * M - 1)
+
+    def acts_copy(k):
+        return remote(
+            acts, acts_all.at[own_slot], acts_ss.at[k], acts_rs.at[t], to_device(dp, lax.rem(t + k, T), s)
+        )
+
+    def acts_arrival(k):
+        z = lax.rem(t + k, T)
+        slot = rows_at((lax.rem(z + s, 2) * 2 + z // 2) * group, group)
+        return remote(acts, acts_all.at[slot], acts_ss.at[k], acts_rs.at[z], across)
+
+    @pl.loop(1, T)
+    def _(k):
+        acts_copy(k).start()
+
+    up_across = remote(
+        up.at[:, pl.ds(there, span)], upbuf.at[group : 2 * group], mat_ss.at[0], mat_rs.at[0], across
+    )
+    up_beside = remote(
+        up.at[:, pl.ds(here, span)], upbuf.at[2 * group : 3 * group], mat_ss.at[1], mat_rs.at[1], sibling
+    )
+    up_forward = remote(
+        upbuf.at[group : 2 * group], upbuf.at[3 * group : 4 * group], mat_ss.at[2], mat_rs.at[2], sibling
+    )
+    rd_across = remote(
+        readout.at[:, pl.ds(there, span)],
+        rd.at[rows_at(dp * group, group)],
+        mat_ss.at[3],
+        mat_rs.at[3],
+        across,
+    )
+    row_lane = lax.broadcasted_iota(jnp.int32, (pairs.shape[0], half), 1) - dp * group
+    pick[dp] = (pairs[:, 0:1] == row_lane).astype(jnp.float32) - (
+        pairs[:, 1:2] == row_lane
+    ).astype(jnp.float32)
+    pick_across = remote(pick.at[dp], pick.at[dp], mat_ss.at[4], mat_rs.at[4], across)
+    pick_arrival = remote(pick.at[1 - dp], pick.at[1 - dp], mat_ss.at[4], mat_rs.at[4], across)
+    rd_arrival = remote(
+        readout.at[:, pl.ds(there, span)],
+        rd.at[rows_at((1 - dp) * group, group)],
+        mat_ss.at[3],
+        mat_rs.at[3],
+        across,
+    )
+    up_across.start()
+    rd_across.start()
+    pick_across.start()
+    up_beside.start()
+
+    @pl.loop(2, 2 * chunks)
+    def _(c):
+        w_copy(c).start()
+
+    acts_local.wait()
+
+    @pl.loop(1, T)
+    def _(k):
+        acts_arrival(k).wait_recv()
+
+    acts_back = pltpu.make_async_copy(acts_all, acts_out, local_sem.at[3])
+    acts_back.start()
+
+    first = [ids[g * group : (g + 1) * group] for g in range(4)]
+    ids_even = jnp.concatenate([first[0], first[2]], axis=0)
+    ids_odd = jnp.concatenate([first[1], first[3]], axis=0)
+    on_odd = jnp.full((half, 1), s, jnp.int32) == 1
+    ids_own = jnp.where(on_odd, ids_odd, ids_even)
+    ids_sib = jnp.where(on_odd, ids_even, ids_odd)
+    ids_all = jnp.concatenate([ids_own, ids_sib], axis=0)
+
+    products = jnp.dot(acts_all[...], down[...], preferred_element_type=jnp.float32)
+    terms[...] = jnp.where(ids_all == t, products, 0.0).astype(jnp.bfloat16)
+
+    def terms_copy(k):
+        number, d, z, c = device_at(k)
+        block = jnp.where(c == s, 0, M) + d * T + z
+        return remote(
+            terms.at[rows_at(block * share, share)],
+            terms_in.at[me],
+            terms_ss.at[number],
+            terms_rs.at[me],
+            to_device(d, z, c),
+        )
+
+    def terms_arrival(k):
+        number, d, z, c = device_at(k)
+        return remote(
+            terms.at[0:share], terms_in.at[number], terms_ss.at[number], terms_rs.at[number], sibling
+        )
+
+    def same_sub(k):
+        number = lax.rem(mine + k, M)
+        return number, number // T, lax.rem(number, T)
+
+    def shrink_copy(k):
+        number, d, z = same_sub(k)
+        return remote(
+            shrink_own,
+            shrink_half.at[rows_at(mine * share, share)],
+            shrink_ss.at[number],
+            shrink_rs.at[mine],
+            to_device(d, z, s),
+        )
+
+    def shrink_arrival(k):
+        number, d, z = same_sub(k)
+        return remote(
+            shrink_own,
+            shrink_half.at[rows_at(number * share, share)],
+            shrink_ss.at[number],
+            shrink_rs.at[number],
+            sibling,
+        )
+
+    @pl.loop(1, 2 * M)
+    def _(k):
+        terms_copy(k).start()
+
+    terms_in[me] = terms[rows_at(mine * share, share)]
+
+    def sib_copy(c):
+        return remote(sib_out.at[c], sib_in.at[c], sib_ss.at[c], sib_rs.at[c], sibling)
+
+    def x_copy(c):
+        return remote(x_out.at[c], x_in.at[c], x_ss.at[c], x_rs.at[c], across)
+
+    def add_sibling(c):
+        sib_copy(c).wait_recv()
+        total = own[c] + sib_in[c].astype(jnp.float32)
+
+        @pl.when(c < chunks)
+        def _():
+            x_out[jnp.minimum(c, chunks - 1)] = total.astype(jnp.bfloat16)
+            x_copy(jnp.minimum(c, chunks - 1)).start()
+
+        @pl.when(c >= chunks)
+        def _():
+            own[c] = total
+
+    @pl.loop(0, 2 * chunks)
+    def _(c):
+        w_copy(c).wait()
+        part = jnp.dot(acts_all[...], wbuf[c], preferred_element_type=jnp.float32)
+        sib_out[c] = part[half:].astype(jnp.bfloat16)
+        sib_copy(c).start()
+        own[c] = part[:half].astype(jnp.bfloat16).astype(jnp.float32)
+
+        @pl.when(c > 0)
+        def _():
+            add_sibling(c - 1)
+
+        @pl.when(c == 2)
+        def _():
+            @pl.loop(1, 2 * M)
+            def _(k):
+                terms_arrival(k).wait_recv()
+
+            low = jnp.sum(terms_in[...].astype(jnp.float32), axis=0).astype(jnp.bfloat16)
+            shrink_own[...] = low
+            shrink_half[rows_at(mine * share, share)] = low
+
+            @pl.loop(1, M)
+            def _(k):
+                shrink_copy(k).start()
+
+    add_sibling(2 * chunks - 1)
+    up_across.wait_recv()
+    up_forward.start()
+
+    @pl.loop(1, M)
+    def _(k):
+        shrink_arrival(k).wait_recv()
+
+    slot_own = (ids_own + s) % 2 * 2 + (ids_own // 2 + dp) % 2
+    low = shrink_half[...]
+    lane_slot = lax.broadcasted_iota(jnp.int32, (half, 4 * rank), 1) // rank
+    scat[...] = jnp.where(
+        slot_own == lane_slot, jnp.concatenate([low] * 4, axis=1).astype(jnp.float32), 0.0
+    ).astype(jnp.bfloat16)
+    up_local.wait()
+    rd_local.wait()
+    up_beside.wait_recv()
+    rd_arrival.wait_recv()
+    up_forward.wait_recv()
+    score_acc[...] = jnp.zeros_like(score_acc)
+
+    def columns_of(j):
+        return pl.ds(pl.multiple_of(j * chunk, 128), chunk)
+
+    @pl.loop(0, chunks)
+    def _(j):
+        x_copy(j).wait_recv()
+        base = own[chunks + j] + x_in[j].astype(jnp.float32)
+        widened = jnp.dot(
+            scat[...], upbuf[:, columns_of(j)], preferred_element_type=jnp.float32
+        ).astype(jnp.bfloat16)
+        policy = base + adapter_scale * widened.astype(jnp.float32)
+        read = rd[:, columns_of(j)].astype(jnp.float32)
+        sig = jax.nn.sigmoid(policy)
+        gain = read * (policy * sig - base * jax.nn.sigmoid(base))
+        total = score_acc[...]
+        for i in range(chunk // 128):
+            total = total + gain[:, i * 128 : (i + 1) * 128]
+        score_acc[...] = total
+        own[chunks + j] = read * (sig * (1.0 + policy * (1.0 - sig)))
+
+    margin_own[...] = jnp.broadcast_to(
+        jnp.sum(score_acc[...].T, axis=0, keepdims=True), margin_own.shape
+    )
+
+    def margin_copy(k):
+        number, d, z = same_sub(k)
+        return remote(
+            margin_own, margin_in.at[mine], margin_ss.at[number], margin_rs.at[mine], to_device(d, z, s)
+        )
+
+    def margin_arrival(k):
+        number, d, z = same_sub(k)
+        return remote(
+            margin_own, margin_in.at[number], margin_ss.at[number], margin_rs.at[number], sibling
+        )
+
+    @pl.loop(1, M)
+    def _(k):
+        margin_copy(k).start()
+
+    margin_in[mine] = margin_own[...]
+    pick_arrival.wait_recv()
+
+    @pl.loop(1, M)
+    def _(k):
+        margin_arrival(k).wait_recv()
+
+    margin_rows = jnp.sum(margin_in[...], axis=0)[0:1]
+    picks = pick[...].reshape(-1, half)
+    margin = beta_pref * jnp.sum(picks * margin_rows, axis=1, keepdims=True)
+    weight = beta_pref * jax.nn.sigmoid(-margin)
+    row_grad = -jnp.sum(picks * weight, axis=0, keepdims=True)
+    row_column = jnp.broadcast_to(row_grad, (half, half)).T[:, 0:1]
+    rank_acc[...] = jnp.zeros_like(rank_acc)
+
+    def ug_copy(j):
+        return remote(ug_out.at[j], ug_in.at[j], ug_ss.at[j], ug_rs.at[j], sibling)
+
+    def gx_copy(j):
+        return remote(gx_out.at[j], gx_in.at[j], gx_ss.at[j], gx_rs.at[j], across)
+
+    def out_copy(j):
+        off = pl.multiple_of(dp * span + j * chunk, 128)
+        return pltpu.make_async_copy(gown.at[j], upg.at[:, pl.ds(off, chunk)], out_sem.at[j])
+
+    def out_copy_across(j):
+        off = pl.multiple_of((1 - dp) * span + j * chunk, 128)
+        return pltpu.make_async_copy(
+            gx_in.at[j], upg.at[:, pl.ds(off, chunk)], out_sem.at[chunks + j]
+        )
+
+    def add_up(j):
+        ug_copy(j).wait_recv()
+        total = (ug_own[j] + ug_in[j].astype(jnp.float32)).astype(jnp.bfloat16)
+        gx_out[j] = total[group:]
+        gx_copy(j).start()
+        gown[j] = total[:group]
+        out_copy(j).start()
+
+    @pl.loop(0, chunks)
+    def _(j):
+        grad = (row_column * own[chunks + j]).astype(jnp.bfloat16)
+        ug = lax.dot_general(
+            scat[...], grad, (((0,), (0,)), ((), ())), preferred_element_type=jnp.float32
+        )
+        ug = adapter_scale * ug
+        ug_out[j] = ug[half:].astype(jnp.bfloat16)
+        ug_copy(j).start()
+        ug_own[j] = ug[:half]
+        rank_acc[...] += lax.dot_general(
+            grad,
+            upbuf[:, columns_of(j)],
+            (((1,), (1,)), ((), ())),
+            preferred_element_type=jnp.float32,
+        )
+
+        @pl.when(j > 0)
+        def _():
+            add_up(j - 1)
+
+    every = jnp.where(slot_own == lane_slot, rank_acc[...], 0.0)
+    rank_part[...] = sum(every[:, i * rank : (i + 1) * rank] for i in range(4))
+
+    def rank_copy(k):
+        number, d, z = same_sub(k)
+        return remote(
+            rank_part.at[rows_at(number * share, share)],
+            rank_in.at[mine],
+            rank_ss.at[number],
+            rank_rs.at[mine],
+            to_device(d, z, s),
+        )
+
+    def rank_arrival(k):
+        number, d, z = same_sub(k)
+        return remote(
+            rank_part.at[0:share], rank_in.at[number], rank_ss.at[number], rank_rs.at[number], sibling
+        )
+
+    @pl.loop(1, M)
+    def _(k):
+        rank_copy(k).start()
+
+    rank_in[mine] = rank_part[rows_at(mine * share, share)]
+    add_up(chunks - 1)
+
+    @pl.loop(1, M)
+    def _(k):
+        rank_arrival(k).wait_recv()
+
+    low = (adapter_scale * jnp.sum(rank_in[...], axis=0)).astype(jnp.bfloat16)
+    rank_own[...] = low
+
+    def all_copy(k):
+        number, d, z, c = device_at(k)
+        block = jnp.where(c == s, 0, M) + mine
+        return remote(
+            rank_own,
+            rank_all.at[rows_at(block * share, share)],
+            all_ss.at[number],
+            all_rs.at[me],
+            to_device(d, z, c),
+        )
+
+    def all_arrival(k):
+        number, d, z, c = device_at(k)
+        block = jnp.where(c == s, 0, M) + d * T + z
+        return remote(
+            rank_own,
+            rank_all.at[rows_at(block * share, share)],
+            all_ss.at[number],
+            all_rs.at[number],
+            sibling,
+        )
+
+    @pl.loop(1, 2 * M)
+    def _(k):
+        all_copy(k).start()
+
+    rank_all[rows_at(mine * share, share)] = low
+
+    @pl.loop(1, 2 * M)
+    def _(k):
+        all_arrival(k).wait_recv()
+
+    rank_out[...] = jnp.where(ids_all == t, rank_all[...].astype(jnp.float32), 0.0).astype(
+        jnp.bfloat16
+    )
+
+    @pl.loop(0, chunks)
+    def _(j):
+        gx_copy(j).wait_recv()
+        out_copy_across(j).start()
+
+    @pl.loop(0, chunks)
+    def _(j):
+        x_copy(j).wait_send()
+        ug_copy(j).wait_send()
+        gx_copy(j).wait_send()
+        out_copy(j).wait()
+        out_copy_across(j).wait()
+
+    @pl.loop(0, 2 * chunks)
+    def _(c):
+        sib_copy(c).wait_send()
+
+    @pl.loop(1, T)
+    def _(k):
+        acts_copy(k).wait_send()
+
+    @pl.loop(1, M)
+    def _(k):
+        shrink_copy(k).wait_send()
+        margin_copy(k).wait_send()
+        rank_copy(k).wait_send()
+
+    @pl.loop(1, 2 * M)
+    def _(k):
+        terms_copy(k).wait_send()
+        all_copy(k).wait_send()
+
+    up_across.wait_send()
+    up_beside.wait_send()
+    up_forward.wait_send()
+    rd_across.wait_send()
+    pick_across.wait_send()
+    acts_back.wait()
+
+
+def fast_body(
+    acts,
+    frozen_weight,
+    adapter_down_maps,
+    adapter_up_maps,
+    down_first_moment,
+    down_second_moment,
+    up_first_moment,
+    up_second_moment,
+    readout,
+    adapter_index_rows,
+    preference_pair_rows,
+):
+    T = lax.axis_size("tensor")
+    group, depth = acts.shape
+    rows = T * group
+    half = rows // 2
+    columns = frozen_weight.shape[1]
+    span = columns // 2
+    rank = adapter_down_maps.shape[2]
+    chunk = chunk_of(span)
+    chunks = span // chunk
+    M = 2 * T
+    share = half // M
+    bf16, f32 = jnp.bfloat16, jnp.float32
+    V, dma = pltpu.VMEM, pltpu.SemaphoreType.DMA
+    any_spec = pl.BlockSpec(memory_space=pl.ANY)
+    vmem_spec = pl.BlockSpec(memory_space=pltpu.VMEM)
+    up_grad, rank_masked, rows_all = pl.pallas_call(
+        functools.partial(step_kernel, T, chunk),
+        out_shape=(
+            jax.ShapeDtypeStruct((rank, columns), bf16),
+            jax.ShapeDtypeStruct((rows, rank), bf16),
+            jax.ShapeDtypeStruct((rows, depth), bf16),
+        ),
+        in_specs=[vmem_spec, any_spec, vmem_spec, any_spec, any_spec, vmem_spec, vmem_spec],
+        out_specs=(any_spec, vmem_spec, any_spec),
+        scratch_shapes=[
+            V((rows, depth), bf16),
+            V((2 * chunks, depth, chunk), bf16),
+            V((2 * chunks, half, chunk), f32),
+            V((2 * chunks, half, chunk), bf16),
+            V((2 * chunks, half, chunk), bf16),
+            V((chunks, half, chunk), bf16),
+            V((chunks, half, chunk), bf16),
+            V((4 * rank, span), bf16),
+            V((half, span), bf16),
+            V((rows, rank), bf16),
+            V((2 * M, share, rank), bf16),
+            V((share, rank), bf16),
+            V((half, rank), bf16),
+            V((half, 4 * rank), bf16),
+            V((2, group // 2, half), f32),
+            V((8, half), f32),
+            V((M, 8, half), f32),
+            V((8, 128), f32),
+            V((chunks, half, chunk), f32),
+            V((chunks, half, chunk), bf16),
+            V((chunks, half, chunk), bf16),
+            V((chunks, group, chunk), bf16),
+            V((chunks, group, chunk), bf16),
+            V((chunks, group, chunk), bf16),
+            V((half, rank), f32),
+            V((M, share, rank), f32),
+            V((share, rank), bf16),
+            V((rows, rank), bf16),
+            V((half, 4 * rank), f32),
+            V((half, 128), f32),
+            dma((T,)), dma((T,)), dma((2 * chunks,)), dma((4,)),
+            dma((2 * chunks,)), dma((2 * chunks,)), dma((chunks,)), dma((chunks,)),
+            dma((5,)), dma((5,)), dma((2 * M,)), dma((2 * M,)),
+            dma((M,)), dma((M,)), dma((M,)), dma((M,)),
+            dma((chunks,)), dma((chunks,)), dma((chunks,)), dma((chunks,)),
+            dma((2 * chunks,)), dma((M,)), dma((M,)), dma((2 * M,)), dma((2 * M,)),
+        ],
+        compiler_params=pltpu.CompilerParams(
+            collective_id=0, has_side_effects=True, vmem_limit_bytes=52 * 1024 * 1024
+        ),
+    )(
+        acts,
+        frozen_weight,
+        adapter_down_maps[0],
+        adapter_up_maps[0],
+        readout,
+        adapter_index_rows,
+        preference_pair_rows,
+    )
+    down_gradient = jnp.einsum("rd,rk->dk", rows_all, rank_masked, preferred_element_type=f32)[None]
+    up_gradient = up_grad.astype(f32)[None]
+    return moment_update_step(
+        adapter_down_maps, down_first_moment, down_second_moment, down_gradient
+    ) + moment_update_step(adapter_up_maps, up_first_moment, up_second_moment, up_gradient)
+
+
+def chunk_of(span):
+    return next((c for c in (640, 512, 384, 256, 128) if span % c == 0), 0)
+
+
+def fits(mesh, args):
+    sizes = mesh.shape
+    T = sizes["tensor"]
+    if sizes["dp"] != 2 or sizes["sub"] != 2 or T != 4:
+        return False
+    rows = args[0].shape[0] // sizes["parts"]
+    span = args[1].shape[1] // (2 * T)
+    rank = args[2].shape[2]
+    return rows == 256 and rank == 64 and args[2].shape[0] == 4 * sizes["parts"] and chunk_of(span) > 0
+
+
 def solution(mesh):
     placed = (
         P(("parts", "tensor"), ("dp", "sub")),
@@ -195,8 +785,11 @@
         P("parts", None),
         P(("parts", "dp", "sub"), None),
     )
-    return jax.shard_map(
-        body,
+    def run(*args):
+        return sharded(fast_body if fits(mesh, args) else body)(*args)
+
+    sharded = lambda inner: jax.shard_map(
+        inner,
         mesh=mesh,
         in_specs=placed,
         out_specs=(
@@ -209,3 +802,4 @@
         ),
         check_vma=False,
     )
+    return run

time: 205 us -> 78.9 us (0.38)
  waiting for transfers between devices: 78.6 us -> 0 us
  Pallas kernels: 0 us -> 68.5 us
  blocking collectives: 68.2 us -> 0 us
  matrix products: 29.4 us -> 1.31 us
  starting transfers between devices: 21.5 us -> 0 us
    all_to_all x6 -> x0, waiting for transfers between devices: 78.6 us -> none  [the longest x1 35.3 us: body(): lax.all_to_all(base_terms, ('dp', 'sub'), split_axis=0, concat_axis=0, ti...]
    pallas_call x0 -> x1, Pallas kernels: none -> 68.5 us  [fast_body(): pl.pallas_call(functools.partial(step_kernel, T, chunk), out_shape=(jax.S...]
    all_gather x3 -> x0, blocking collectives: 41.4 us -> none  [the longest x1 19.8 us: body(): rows_all = lax.all_gather(acts, 'tensor', axis=0, tiled=True)]
    dot_general x9 -> x1, matrix products: 29 us -> 1.31 us  [fast_body(): jnp.einsum('rd,rk->dk', rows_all, rank_masked, preferred_element_type=f32)]
    psum x2 -> x0, blocking collectives: 26.8 us -> none  [the longest x1 15.8 us: body(): lax.psum(rank_portion, 'tensor')]
    all_to_all x6 -> x0, starting transfers between devices: 21.5 us -> none  [the longest x1 4.34 us: body(): lax.all_to_all(expanded.reshape(group_count * local_up_maps, slot_count,...]
    convert_element_type x3 -> x1, other arithmetic: 0.09 us -> 3.86 us  [moment_update_step(): (param.astype(jnp.float32) - learn_rate * update_step).astype(jnp.bfloat16)]
    reduce_sum x6 -> x0, other arithmetic: 2.14 us -> none  [the longest x1 1.64 us: body(): frozen_sum = jnp.sum(base_arrived.astype(jnp.float32), axis=0)]
  transfers between devices with their start and end apart: 6 -> 0, of which waited for: 4 -> 0; matrix products, arithmetic and copies ran while one was open for 11% -> 0% of each run, Pallas kernels for 0% -> 0%
where the time goes in v1:
time: 78.9 us; the launch traced here: 78.6 us
  Pallas kernels  68.5 us (87%)
  local copies, waits for them, and re-layouts  4.26 us (5%)
  other arithmetic  3.86 us (5%)
  matrix products  1.31 us (2%)
    pallas_call x1, Pallas kernels, fast_body(): pl.pallas_call(functools.partial(step_kernel, T, chunk), out_shape=(jax.S...  68.5 us
    unnamed x17, local copies, waits for them, and re-layouts  4.26 us
    convert_element_type x1, other arithmetic, moment_update_step(): (param.astype(jnp.float32) - learn_rate * update_step).astype(jnp.bfloat16)  3.86 us

profile of v1, /device:TPU:0, one launch (start us, length us, event | category | flops | bytes accessed | tf_op | source)
XLA Modules:
  0.0 78.6 jit_solution(14768476899607129446)
XLA Ops:
  0.6 0.8 copy.19.pairs
  1.4 0.8 %copy.18.ids = s32[256,1]{1,0:T(8,128)S(1)} copy(s32[256,1]{0,1:T(1,128)} %param.20) | data formatting | bytes 2048 | tf_op args[9]
  2.2 1.1 %copy.17 = bf16[1,1280,64]{2,1,0:T(8,128)(2,1)S(1)} copy(bf16[1,1280,64]{1,2,0:T(8,128)(2,1)} %param.13) | data formatting | bytes 327680 | tf_op args[2]
  3.3 0.0 copy-start
  3.4 0.9 %copy-done = bf16[64,1280]{1,0:T(8,128)(2,1)S(1)} copy-done((bf16[64,1280]{1,0:T(8,128)(2,1)S(1)}, bf16[64,1280]{1,0:T(8,128)(2,1)}, u32[]{:S(2)}) %copy-start) | copy-done | bytes 163864
  4.3 0.0 copy-start.4
  4.3 0.0 copy-start.5
  4.3 0.0 copy-start.6
  4.3 0.0 copy-start.3
  4.3 68.5 %shard_map.154 = (bf16[64,6400]{1,0:T(8,128)(2,1)}, bf16[256,64]{1,0:T(8,128)(2,1)S(1)}, bf16[256,1280]{1,0:T(8,128)(2,1)S(1)}) custom-call(bf16[64,1280]{1,0:T(8,128)(2,1)S(1)} %copy-done, bf16[1280,6400]{1,0:T(8,128)(2,1)} %w.1, bf16[1280,64]{1,0:T(8,128)(2,1)S(1)} %bitcast.22, bf16[64,6400]{1,0:T(8,128)(2,1)} %bitcast.23, bf16[64,6400]{1,0:T(8,128)(2,1)} %readout.1, ...), custom_call_target="tpu_custom_call" | custom-call | tf_op jit(solution)/shard_map/pallas_call | solution.py:693
  72.7 0.0 copy-start.1
  72.8 0.0 copy-start.2
  72.8 0.0 copy-done.4
  72.8 0.0 copy-done.5
  72.8 0.0 copy-done.6
  72.8 1.3 %subtract_convert_fusion.1 = (bf16[1,1280,64]{1,2,0:T(8,128)(2,1)}, f32[1,1280,64]{1,2,0:T(8,128)}, f32[1,1280,64]{1,2,0:T(8,128)}) fusion(bf16[1,1280,64]{1,2,0:T(8,128)(2,1)S(1)} %copy-done.4, f32[1,1280,64]{1,2,0:T(8,128)S(1)} %copy-done.5, f32[1,1280,64]{1,2,0:T(8,128)S(1)} %copy-done.6, bf16[256,1280]{1,0:T(8,128)(2,1)S(1)} %get-tuple-element.9, ...), kind=kOutput, calls=%fused_computation.11 | convolution fusion | flops 43171840 | bytes 2326528 | tf_op jit(solution)/shard_map/rd,rk->dk/dot_general | solution.py:752
  74.1 0.0 copy-done.3
  74.1 0.0 copy-done.1
  74.1 0.6 copy-done.2
  74.7 3.9 %subtract_convert_fusion = (bf16[1,64,6400]{2,1,0:T(8,128)(2,1)}, f32[1,64,6400]{2,1,0:T(8,128)}, f32[1,64,6400]{2,1,0:T(8,128)}) fusion(bf16[1,64,6400]{2,1,0:T(8,128)(2,1)S(1)} %copy-done.1, bf16[64,6400]{1,0:T(8,128)(2,1)} %get-tuple-element.11, f32[1,64,6400]{2,1,0:T(8,128)S(1)} %copy-done.2, f32[1,64,6400]{2,1,0:T(8,128)S(1)} %copy-done.3), kind=kLoop, calls=%fused_computation.6 | loop fusion | flops 6553600 | bytes 9011200 | tf_op jit(solution)/shard_map/convert_element_type | solution.py:29
Async XLA Ops:
  3.3 0.9 %copy-start = (bf16[64,1280]{1,0:T(8,128)(2,1)S(1)}, bf16[64,1280]{1,0:T(8,128)(2,1)}, u32[]{:S(2)}) copy-start(bf16[64,1280]{1,0:T(8,128)(2,1)} %acts.1) | copy-start | bytes 491524
  4.3 68.5 %copy-start.4 = (bf16[1,1280,64]{1,2,0:T(8,128)(2,1)S(1)}, bf16[1,1280,64]{1,2,0:T(8,128)(2,1)}, u32[]{:S(2)}) copy-start(bf16[1,1280,64]{1,2,0:T(8,128)(2,1)} %param.13) | copy-start | bytes 491524
  4.3 68.5 %copy-start.5 = (f32[1,1280,64]{1,2,0:T(8,128)S(1)}, f32[1,1280,64]{1,2,0:T(8,128)}, u32[]{:S(2)}) copy-start(f32[1,1280,64]{1,2,0:T(8,128)} %param.15) | copy-start | bytes 983044
  4.3 68.5 %copy-start.6 = (f32[1,1280,64]{1,2,0:T(8,128)S(1)}, f32[1,1280,64]{1,2,0:T(8,128)}, u32[]{:S(2)}) copy-start(f32[1,1280,64]{1,2,0:T(8,128)} %param.16) | copy-start | bytes 983044
  4.3 69.8 %copy-start.3 = (f32[1,64,6400]{2,1,0:T(8,128)S(1)}, f32[1,64,6400]{2,1,0:T(8,128)}, u32[]{:S(2)}) copy-start(f32[1,64,6400]{2,1,0:T(8,128)} %param.18) | copy-start | bytes 4915204
  72.7 1.4 %copy-start.1 = (bf16[1,64,6400]{2,1,0:T(8,128)(2,1)S(1)}, bf16[1,64,6400]{2,1,0:T(8,128)(2,1)}, u32[]{:S(2)}) copy-start(bf16[1,64,6400]{2,1,0:T(8,128)(2,1)} %param.14) | copy-start | bytes 2457604
  72.8 2.0 %copy-start.2 = (f32[1,64,6400]{2,1,0:T(8,128)S(1)}, f32[1,64,6400]{2,1,0:T(8,128)}, u32[]{:S(2)}) copy-start(f32[1,64,6400]{2,1,0:T(8,128)} %param.17) | copy-start | bytes 4915204

commit v2 on v1

--- a/solution.py
+++ b/solution.py
@@ -205,12 +205,12 @@
 
 
 def step_kernel(
-    T, chunk, acts, w, down, up, readout, ids, pairs,
+    T, chunk, acts, w, down_in, up, readout, ids_in, pairs_in,
     upg, rank_out, acts_out,
     acts_all, wbuf, own, sib_out, sib_in, x_out, x_in, upbuf, rd,
     terms, terms_in, shrink_own, shrink_half, scat, pick,
     margin_own, margin_in, grad_out, ug_own, ug_out, ug_in, gx_out, gx_in, gown,
-    rank_part, rank_in, rank_own, rank_all, rank_acc, score_acc,
+    rank_part, rank_in, rank_own, rank_all, rank_acc, score_acc, down, ids, pairs, grads,
     acts_ss, acts_rs, w_sem, local_sem, sib_ss, sib_rs, x_ss, x_rs,
     mat_ss, mat_rs, terms_ss, terms_rs, shrink_ss, shrink_rs, margin_ss, margin_rs,
     ug_ss, ug_rs, gx_ss, gx_rs, out_sem, rank_ss, rank_rs, all_ss, all_rs,
@@ -222,8 +222,8 @@
     columns = w.shape[1]
     span = columns // 2
     chunks = span // chunk
-    rank = down.shape[1]
-    share = half // (2 * T)
+    rank = down.shape[0]
+    share = half // T
     M = 2 * T
     mine = dp * T + t
     me = mine * 2 + s
@@ -243,6 +243,13 @@
         number = lax.rem(me + k, 2 * M)
         return number, number // (2 * T), lax.rem(number // 2, T), lax.rem(number, 2)
 
+    ids_local = pltpu.make_async_copy(ids_in, ids, local_sem.at[4])
+    pairs_local = pltpu.make_async_copy(pairs_in, pairs, local_sem.at[5])
+    down_local = pltpu.make_async_copy(down_in, down, local_sem.at[6])
+    ids_local.start()
+    pairs_local.start()
+    down_local.start()
+
     @pl.loop(0, 2)
     def _(c):
         w_copy(c).start()
@@ -268,19 +275,43 @@
 
     pl.semaphore_wait(barrier, 2 * M - 1)
 
-    def acts_copy(k):
-        return remote(
-            acts, acts_all.at[own_slot], acts_ss.at[k], acts_rs.at[t], to_device(dp, lax.rem(t + k, T), s)
-        )
-
-    def acts_arrival(k):
-        z = lax.rem(t + k, T)
-        slot = rows_at((lax.rem(z + s, 2) * 2 + z // 2) * group, group)
-        return remote(acts, acts_all.at[slot], acts_ss.at[k], acts_rs.at[z], across)
-
-    @pl.loop(1, T)
-    def _(k):
-        acts_copy(k).start()
+    def acts_slot(z):
+        return acts_all.at[rows_at((lax.rem(z + s, 2) * 2 + z // 2) * group, group)]
+
+    def acts_up(i):
+        block = t - i
+        return remote(
+            acts_slot(block), acts_slot(block), acts_ss.at[i], acts_rs.at[block], to_device(dp, t + 1, s)
+        )
+
+    def acts_downward(i):
+        block = t + i
+        return remote(
+            acts_slot(block),
+            acts_slot(block),
+            acts_ss.at[T + i],
+            acts_rs.at[block],
+            to_device(dp, t - 1, s),
+        )
+
+    def acts_arrival(block):
+        return remote(acts_slot(block), acts_slot(block), acts_ss.at[0], acts_rs.at[block], sibling)
+
+    def when_up(i):
+        return (t - i >= 0) & (t + 1 < T)
+
+    def when_down(i):
+        return (t + i < T) & (t >= 1)
+
+    acts_local.wait()
+
+    @pl.when(when_up(0))
+    def _():
+        acts_up(0).start()
+
+    @pl.when(when_down(0))
+    def _():
+        acts_downward(0).start()
 
     up_across = remote(
         up.at[:, pl.ds(there, span)], upbuf.at[group : 2 * group], mat_ss.at[0], mat_rs.at[0], across
@@ -298,10 +329,6 @@
         mat_rs.at[3],
         across,
     )
-    row_lane = lax.broadcasted_iota(jnp.int32, (pairs.shape[0], half), 1) - dp * group
-    pick[dp] = (pairs[:, 0:1] == row_lane).astype(jnp.float32) - (
-        pairs[:, 1:2] == row_lane
-    ).astype(jnp.float32)
     pick_across = remote(pick.at[dp], pick.at[dp], mat_ss.at[4], mat_rs.at[4], across)
     pick_arrival = remote(pick.at[1 - dp], pick.at[1 - dp], mat_ss.at[4], mat_rs.at[4], across)
     rd_arrival = remote(
@@ -313,23 +340,22 @@
     )
     up_across.start()
     rd_across.start()
-    pick_across.start()
     up_beside.start()
 
     @pl.loop(2, 2 * chunks)
     def _(c):
         w_copy(c).start()
 
-    acts_local.wait()
-
-    @pl.loop(1, T)
-    def _(k):
-        acts_arrival(k).wait_recv()
-
-    acts_back = pltpu.make_async_copy(acts_all, acts_out, local_sem.at[3])
-    acts_back.start()
-
-    first = [ids[g * group : (g + 1) * group] for g in range(4)]
+    pairs_local.wait()
+    row_line = lax.broadcasted_iota(jnp.int32, (half, group // 2), 0) - dp * group
+    pick[dp] = (
+        (pairs[0:1] == row_line).astype(jnp.float32) - (pairs[1:2] == row_line).astype(jnp.float32)
+    ).T
+    pick_across.start()
+    ids_local.wait()
+    ids_column = jnp.broadcast_to(ids[...].astype(jnp.float32), (128, rows)).T[:, 0:1]
+    ids_column = ids_column.astype(jnp.int32)
+    first = [ids_column[g * group : (g + 1) * group] for g in range(4)]
     ids_even = jnp.concatenate([first[0], first[2]], axis=0)
     ids_odd = jnp.concatenate([first[1], first[3]], axis=0)
     on_odd = jnp.full((half, 1), s, jnp.int32) == 1
@@ -337,12 +363,36 @@
     ids_sib = jnp.where(on_odd, ids_even, ids_odd)
     ids_all = jnp.concatenate([ids_own, ids_sib], axis=0)
 
-    products = jnp.dot(acts_all[...], down[...], preferred_element_type=jnp.float32)
+    down_local.wait()
+
+    @pl.loop(1, T)
+    def _(i):
+        @pl.when(t - i >= 0)
+        def _():
+            acts_arrival(t - i).wait_recv()
+
+            @pl.when(when_up(i))
+            def _():
+                acts_up(i).start()
+
+        @pl.when(t + i < T)
+        def _():
+            acts_arrival(t + i).wait_recv()
+
+            @pl.when(when_down(i))
+            def _():
+                acts_downward(i).start()
+
+    acts_back = pltpu.make_async_copy(acts_all, acts_out, local_sem.at[3])
+    acts_back.start()
+    products = lax.dot_general(
+        acts_all[...], down[...], (((1,), (1,)), ((), ())), preferred_element_type=jnp.float32
+    )
     terms[...] = jnp.where(ids_all == t, products, 0.0).astype(jnp.bfloat16)
 
     def terms_copy(k):
         number, d, z, c = device_at(k)
-        block = jnp.where(c == s, 0, M) + d * T + z
+        block = jnp.where(c == s, 0, T) + z
         return remote(
             terms.at[rows_at(block * share, share)],
             terms_in.at[me],
@@ -362,22 +412,22 @@
         return number, number // T, lax.rem(number, T)
 
     def shrink_copy(k):
-        number, d, z = same_sub(k)
+        z = lax.rem(t + k, T)
         return remote(
             shrink_own,
-            shrink_half.at[rows_at(mine * share, share)],
-            shrink_ss.at[number],
-            shrink_rs.at[mine],
-            to_device(d, z, s),
+            shrink_half.at[rows_at(t * share, share)],
+            shrink_ss.at[z],
+            shrink_rs.at[t],
+            to_device(dp, z, s),
         )
 
     def shrink_arrival(k):
-        number, d, z = same_sub(k)
+        z = lax.rem(t + k, T)
         return remote(
             shrink_own,
-            shrink_half.at[rows_at(number * share, share)],
-            shrink_ss.at[number],
-            shrink_rs.at[number],
+            shrink_half.at[rows_at(z * share, share)],
+            shrink_ss.at[z],
+            shrink_rs.at[z],
             sibling,
         )
 
@@ -385,7 +435,7 @@
     def _(k):
         terms_copy(k).start()
 
-    terms_in[me] = terms[rows_at(mine * share, share)]
+    terms_in[me] = terms[rows_at(t * share, share)]
 
     def sib_copy(c):
         return remote(sib_out.at[c], sib_in.at[c], sib_ss.at[c], sib_rs.at[c], sibling)
@@ -426,9 +476,9 @@
 
             low = jnp.sum(terms_in[...].astype(jnp.float32), axis=0).astype(jnp.bfloat16)
             shrink_own[...] = low
-            shrink_half[rows_at(mine * share, share)] = low
-
-            @pl.loop(1, M)
+            shrink_half[rows_at(t * share, share)] = low
+
+            @pl.loop(1, T)
             def _(k):
                 shrink_copy(k).start()
 
@@ -436,7 +486,7 @@
     up_across.wait_recv()
     up_forward.start()
 
-    @pl.loop(1, M)
+    @pl.loop(1, T)
     def _(k):
         shrink_arrival(k).wait_recv()
 
@@ -494,6 +544,39 @@
         margin_copy(k).start()
 
     margin_in[mine] = margin_own[...]
+
+    @pl.loop(0, chunks)
+    def _(j):
+        x_copy(j).wait_send()
+
+    @pl.loop(0, 2 * chunks)
+    def _(c):
+        sib_copy(c).wait_send()
+
+    @pl.loop(0, T - 1)
+    def _(i):
+        @pl.when(when_up(i))
+        def _():
+            acts_up(i).wait_send()
+
+        @pl.when(when_down(i))
+        def _():
+            acts_downward(i).wait_send()
+
+    @pl.loop(1, T)
+    def _(k):
+        shrink_copy(k).wait_send()
+
+    @pl.loop(1, 2 * M)
+    def _(k):
+        terms_copy(k).wait_send()
+
+    up_across.wait_send()
+    up_beside.wait_send()
+    up_forward.wait_send()
+    rd_across.wait_send()
+    pick_across.wait_send()
+    acts_back.wait()
     pick_arrival.wait_recv()
 
     @pl.loop(1, M)
@@ -535,13 +618,7 @@
     @pl.loop(0, chunks)
     def _(j):
         grad = (row_column * own[chunks + j]).astype(jnp.bfloat16)
-        ug = lax.dot_general(
-            scat[...], grad, (((0,), (0,)), ((), ())), preferred_element_type=jnp.float32
-        )
-        ug = adapter_scale * ug
-        ug_out[j] = ug[half:].astype(jnp.bfloat16)
-        ug_copy(j).start()
-        ug_own[j] = ug[:half]
+        grads[j] = grad
         rank_acc[...] += lax.dot_general(
             grad,
             upbuf[:, columns_of(j)],
@@ -549,17 +626,13 @@
             preferred_element_type=jnp.float32,
         )
 
-        @pl.when(j > 0)
-        def _():
-            add_up(j - 1)
-
     every = jnp.where(slot_own == lane_slot, rank_acc[...], 0.0)
     rank_part[...] = sum(every[:, i * rank : (i + 1) * rank] for i in range(4))
 
     def rank_copy(k):
         number, d, z = same_sub(k)
         return remote(
-            rank_part.at[rows_at(number * share, share)],
+            rank_part.at[rows_at(z * share, share)],
             rank_in.at[mine],
             rank_ss.at[number],
             rank_rs.at[mine],
@@ -576,7 +649,22 @@
     def _(k):
         rank_copy(k).start()
 
-    rank_in[mine] = rank_part[rows_at(mine * share, share)]
+    rank_in[mine] = rank_part[rows_at(t * share, share)]
+
+    @pl.loop(0, chunks)
+    def _(j):
+        ug = lax.dot_general(
+            scat[...], grads[j], (((0,), (0,)), ((), ())), preferred_element_type=jnp.float32
+        )
+        ug = adapter_scale * ug
+        ug_out[j] = ug[half:].astype(jnp.bfloat16)
+        ug_copy(j).start()
+        ug_own[j] = ug[:half]
+
+        @pl.when(j > 0)
+        def _():
+            add_up(j - 1)
+
     add_up(chunks - 1)
 
     @pl.loop(1, M)
@@ -586,20 +674,24 @@
     low = (adapter_scale * jnp.sum(rank_in[...], axis=0)).astype(jnp.bfloat16)
     rank_own[...] = low
 
+    def on_side(k):
+        number = lax.rem(t * 2 + s + k, M)
+        return number, number // 2, lax.rem(number, 2)
+
     def all_copy(k):
-        number, d, z, c = device_at(k)
-        block = jnp.where(c == s, 0, M) + mine
+        number, z, c = on_side(k)
+        block = jnp.where(c == s, 0, T) + t
         return remote(
             rank_own,
             rank_all.at[rows_at(block * share, share)],
             all_ss.at[number],
-            all_rs.at[me],
-            to_device(d, z, c),
+            all_rs.at[t * 2 + s],
+            to_device(dp, z, c),
         )
 
     def all_arrival(k):
-        number, d, z, c = device_at(k)
-        block = jnp.where(c == s, 0, M) + d * T + z
+        number, z, c = on_side(k)
+        block = jnp.where(c == s, 0, T) + z
         return remote(
             rank_own,
             rank_all.at[rows_at(block * share, share)],
@@ -608,15 +700,28 @@
             sibling,
         )
 
-    @pl.loop(1, 2 * M)
+    @pl.loop(1, M)
     def _(k):
         all_copy(k).start()
 
-    rank_all[rows_at(mine * share, share)] = low
-
-    @pl.loop(1, 2 * M)
+    rank_all[rows_at(t * share, share)] = low
+
+    @pl.loop(1, M)
+    def _(k):
+        margin_copy(k).wait_send()
+        rank_copy(k).wait_send()
+
+    @pl.loop(0, chunks)
+    def _(j):
+        ug_copy(j).wait_send()
+
+    @pl.loop(1, M)
     def _(k):
         all_arrival(k).wait_recv()
+
+    @pl.loop(1, M)
+    def _(k):
+        all_copy(k).wait_send()
 
     rank_out[...] = jnp.where(ids_all == t, rank_all[...].astype(jnp.float32), 0.0).astype(
         jnp.bfloat16
@@ -629,37 +734,9 @@
 
     @pl.loop(0, chunks)
     def _(j):
-        x_copy(j).wait_send()
-        ug_copy(j).wait_send()
         gx_copy(j).wait_send()
         out_copy(j).wait()
         out_copy_across(j).wait()
-
-    @pl.loop(0, 2 * chunks)
-    def _(c):
-        sib_copy(c).wait_send()
-
-    @pl.loop(1, T)
-    def _(k):
-        acts_copy(k).wait_send()
-
-    @pl.loop(1, M)
-    def _(k):
-        shrink_copy(k).wait_send()
-        margin_copy(k).wait_send()
-        rank_copy(k).wait_send()
-
-    @pl.loop(1, 2 * M)
-    def _(k):
-        terms_copy(k).wait_send()
-        all_copy(k).wait_send()
-
-    up_across.wait_send()
-    up_beside.wait_send()
-    up_forward.wait_send()
-    rd_across.wait_send()
-    pick_across.wait_send()
-    acts_back.wait()
 
 
 def fast_body(
@@ -685,7 +762,7 @@
     chunk = chunk_of(span)
     chunks = span // chunk
     M = 2 * T
-    share = half // M
+    share = half // T
     bf16, f32 = jnp.bfloat16, jnp.float32
     V, dma = pltpu.VMEM, pltpu.SemaphoreType.DMA
     any_spec = pl.BlockSpec(memory_space=pl.ANY)
@@ -697,7 +774,7 @@
             jax.ShapeDtypeStruct((rows, rank), bf16),
             jax.ShapeDtypeStruct((rows, depth), bf16),
         ),
-        in_specs=[vmem_spec, any_spec, vmem_spec, any_spec, any_spec, vmem_spec, vmem_spec],
+        in_specs=[any_spec] * 7,
         out_specs=(any_spec, vmem_spec, any_spec),
         scratch_shapes=[
             V((rows, depth), bf16),
@@ -730,24 +807,33 @@
             V((rows, rank), bf16),
             V((half, 4 * rank), f32),
             V((half, 128), f32),
-            dma((T,)), dma((T,)), dma((2 * chunks,)), dma((4,)),
+            V((rank, depth), bf16),
+            V((1, rows), jnp.int32),
+            V((2, group // 2), jnp.int32),
+            V((chunks, half, chunk), bf16),
+            dma((2 * T,)), dma((T,)), dma((2 * chunks,)), dma((7,)),
             dma((2 * chunks,)), dma((2 * chunks,)), dma((chunks,)), dma((chunks,)),
             dma((5,)), dma((5,)), dma((2 * M,)), dma((2 * M,)),
-            dma((M,)), dma((M,)), dma((M,)), dma((M,)),
+            dma((T,)), dma((T,)), dma((M,)), dma((M,)),
             dma((chunks,)), dma((chunks,)), dma((chunks,)), dma((chunks,)),
-            dma((2 * chunks,)), dma((M,)), dma((M,)), dma((2 * M,)), dma((2 * M,)),
+            dma((2 * chunks,)), dma((M,)), dma((M,)), dma((M,)), dma((M,)),
         ],
         compiler_params=pltpu.CompilerParams(
-            collective_id=0, has_side_effects=True, vmem_limit_bytes=52 * 1024 * 1024
+            collective_id=0, has_side_effects=True, vmem_limit_bytes=40 * 1024 * 1024
         ),
     )(
-        acts,
-        frozen_weight,
-        adapter_down_maps[0],
-        adapter_up_maps[0],
-        readout,
-        adapter_index_rows,
-        preference_pair_rows,
+        *(
+            pltpu.with_memory_space_constraint(held, pltpu.HBM)
+            for held in (
+                acts,
+                frozen_weight,
+                adapter_down_maps[0].T,
+                adapter_up_maps[0],
+                readout,
+                adapter_index_rows.T,
+                preference_pair_rows.T,
+            )
+        )
     )
     down_gradient = jnp.einsum("rd,rk->dk", rows_all, rank_masked, preferred_element_type=f32)[None]
     up_gradient = up_grad.astype(f32)[None]

time: 78.9 us -> 70.4 us (0.89)
  local copies, waits for them, and re-layouts: 4.26 us -> 0.64 us
  Pallas kernels: 68.5 us -> 64.9 us
  other arithmetic: 3.86 us -> 2.71 us
    unnamed x17 -> x12, local copies, waits for them, and re-layouts: 4.26 us -> 0.64 us
    pallas_call x1, Pallas kernels: 68.5 us -> 64.9 us  [fast_body(): pl.pallas_call(functools.partial(step_kernel, T, chunk), out_shape=(jax.S...]
    convert_element_type x1, other arithmetic: 3.86 us -> 2.71 us  [moment_update_step(): (param.astype(jnp.float32) - learn_rate * update_step).astype(jnp.bfloat16)]
where the time goes in v2:
time: 70.4 us; the launch traced here: 70.2 us
  Pallas kernels  64.9 us (92%)
  other arithmetic  2.71 us (4%)
  matrix products  1.31 us (2%)
  between operations  0.72 us (1%)
    pallas_call x1, Pallas kernels, fast_body(): pl.pallas_call(functools.partial(step_kernel, T, chunk), out_shape=(jax.S...  64.9 us
    convert_element_type x1, other arithmetic, moment_update_step(): (param.astype(jnp.float32) - learn_rate * update_step).astype(jnp.bfloat16)  2.71 us

profile of v2, /device:TPU:0, one launch (start us, length us, event | category | flops | bytes accessed | tf_op | source)
XLA Modules:
  0.0 70.2 jit_solution(2209785207850124378)
XLA Ops:
  0.6 0.0 copy-start.3
  0.6 0.0 copy-start.4
  0.7 0.0 copy-start.5
  0.7 0.0 copy-start.2
  0.7 64.9 %shard_map.154 = (bf16[64,6400]{1,0:T(8,128)(2,1)S(1)}, bf16[256,64]{1,0:T(8,128)(2,1)S(1)}, bf16[256,1280]{1,0:T(8,128)(2,1)S(1)}) custom-call(bf16[64,1280]{1,0:T(8,128)(2,1)} %acts.1, bf16[1280,6400]{1,0:T(8,128)(2,1)} %w.1, bf16[64,1280]{1,0:T(8,128)(2,1)} %bitcast.27, bf16[64,6400]{1,0:T(8,128)(2,1)} %bitcast.26, bf16[64,6400]{1,0:T(8,128)(2,1)} %readout.1, ...), custom_call_target="tpu_custom_call" | custom-call | tf_op jit(solution)/shard_map/pallas_call | solution.py:770
  65.5 0.0 copy-start
  65.5 0.0 copy-start.1
  65.6 0.0 copy-done.3
  65.6 0.0 copy-done.4
  65.6 0.0 copy-done.5
  65.6 1.3 %subtract_convert_fusion.1 = (bf16[1,1280,64]{1,2,0:T(8,128)(2,1)}, f32[1,1280,64]{1,2,0:T(8,128)}, f32[1,1280,64]{1,2,0:T(8,128)}) fusion(bf16[1,1280,64]{1,2,0:T(8,128)(2,1)S(1)} %copy-done.3, f32[1,1280,64]{1,2,0:T(8,128)S(1)} %copy-done.4, f32[1,1280,64]{1,2,0:T(8,128)S(1)} %copy-done.5, bf16[256,1280]{1,0:T(8,128)(2,1)S(1)} %get-tuple-element.9, ...), kind=kOutput, calls=%fused_computation.11 | convolution fusion | flops 43171840 | bytes 2326528 | tf_op jit(solution)/shard_map/rd,rk->dk/dot_general | solution.py:838
  66.9 0.0 copy-done.2
  66.9 0.0 copy-done
  66.9 0.6 copy-done.1
  67.5 2.7 %subtract_convert_fusion = (bf16[1,64,6400]{2,1,0:T(8,128)(2,1)}, f32[1,64,6400]{2,1,0:T(8,128)}, f32[1,64,6400]{2,1,0:T(8,128)}) fusion(bf16[1,64,6400]{2,1,0:T(8,128)(2,1)S(1)} %copy-done, bf16[64,6400]{1,0:T(8,128)(2,1)S(1)} %get-tuple-element.11, f32[1,64,6400]{2,1,0:T(8,128)S(1)} %copy-done.1, f32[1,64,6400]{2,1,0:T(8,128)S(1)} %copy-done.2), kind=kLoop, calls=%fused_computation.6 | loop fusion | flops 6553600 | bytes 9011200 | tf_op jit(solution)/shard_map/convert_element_type | solution.py:29
Async XLA Ops:
  0.6 64.9 %copy-start.3 = (bf16[1,1280,64]{1,2,0:T(8,128)(2,1)S(1)}, bf16[1,1280,64]{1,2,0:T(8,128)(2,1)}, u32[]{:S(2)}) copy-start(bf16[1,1280,64]{1,2,0:T(8,128)(2,1)} %param.13) | copy-start | bytes 491524
  0.6 64.9 %copy-start.4 = (f32[1,1280,64]{1,2,0:T(8,128)S(1)}, f32[1,1280,64]{1,2,0:T(8,128)}, u32[]{:S(2)}) copy-start(f32[1,1280,64]{1,2,0:T(8,128)} %param.15) | copy-start | bytes 983044
  0.7 64.9 %copy-start.5 = (f32[1,1280,64]{1,2,0:T(8,128)S(1)}, f32[1,1280,64]{1,2,0:T(8,128)}, u32[]{:S(2)}) copy-start(f32[1,1280,64]{1,2,0:T(8,128)} %param.16) | copy-start | bytes 983044
  0.7 66.2 %copy-start.2 = (f32[1,64,6400]{2,1,0:T(8,128)S(1)}, f32[1,64,6400]{2,1,0:T(8,128)}, u32[]{:S(2)}) copy-start(f32[1,64,6400]{2,1,0:T(8,128)} %param.18) | copy-start | bytes 4915204
  65.5 1.4 %copy-start = (bf16[1,64,6400]{2,1,0:T(8,128)(2,1)S(1)}, bf16[1,64,6400]{2,1,0:T(8,128)(2,1)}, u32[]{:S(2)}) copy-start(bf16[1,64,6400]{2,1,0:T(8,128)(2,1)} %param.14) | copy-start | bytes 2457604
  65.5 2.0 %copy-start.1 = (f32[1,64,6400]{2,1,0:T(8,128)S(1)}, f32[1,64,6400]{2,1,0:T(8,128)}, u32[]{:S(2)}) copy-start(f32[1,64,6400]{2,1,0:T(8,128)} %param.17) | copy-start | bytes 4915204

commit v3 on v2

--- a/solution.py
+++ b/solution.py
@@ -615,6 +615,18 @@
         gown[j] = total[:group]
         out_copy(j).start()
 
+    def up_part(j):
+        ug = lax.dot_general(
+            scat[...], grads[j], (((0,), (0,)), ((), ())), preferred_element_type=jnp.float32
+        )
+        ug = adapter_scale * ug
+        ug_out[j] = ug[half:].astype(jnp.bfloat16)
+        ug_copy(j).start()
+        ug_own[j] = ug[:half]
+
+    grads[0] = (row_column * own[chunks]).astype(jnp.bfloat16)
+    up_part(0)
+
     @pl.loop(0, chunks)
     def _(j):
         grad = (row_column * own[chunks + j]).astype(jnp.bfloat16)
@@ -651,17 +663,13 @@
 
     rank_in[mine] = rank_part[rows_at(t * share, share)]
 
-    @pl.loop(0, chunks)
+    add_up(0)
+
+    @pl.loop(1, chunks)
     def _(j):
-        ug = lax.dot_general(
-            scat[...], grads[j], (((0,), (0,)), ((), ())), preferred_element_type=jnp.float32
-        )
-        ug = adapter_scale * ug
-        ug_out[j] = ug[half:].astype(jnp.bfloat16)
-        ug_copy(j).start()
-        ug_own[j] = ug[:half]
-
-        @pl.when(j > 0)
+        up_part(j)
+
+        @pl.when(j > 1)
         def _():
             add_up(j - 1)
 

time: 70.4 us -> 70 us (level)
  no operation moved by 1% of the time
where the time goes in v3:
time: 70 us; the launch traced here: 69.8 us
  Pallas kernels  64.4 us (92%)
  other arithmetic  2.71 us (4%)
  matrix products  1.31 us (2%)
  between operations  0.72 us (1%)
    pallas_call x1, Pallas kernels, fast_body(): pl.pallas_call(functools.partial(step_kernel, T, chunk), out_shape=(jax.S...  64.4 us
    convert_element_type x1, other arithmetic, moment_update_step(): (param.astype(jnp.float32) - learn_rate * update_step).astype(jnp.bfloat16)  2.71 us

profile of v3, /device:TPU:0, one launch (start us, length us, event | category | flops | bytes accessed | tf_op | source)
XLA Modules:
  0.0 69.8 jit_solution(377139267904232211)
XLA Ops:
  0.6 0.0 copy-start.3
  0.6 0.0 copy-start.4
  0.7 0.0 copy-start.5
  0.7 0.0 copy-start.2
  0.7 64.4 %shard_map.154 = (bf16[64,6400]{1,0:T(8,128)(2,1)S(1)}, bf16[256,64]{1,0:T(8,128)(2,1)S(1)}, bf16[256,1280]{1,0:T(8,128)(2,1)S(1)}) custom-call(bf16[64,1280]{1,0:T(8,128)(2,1)} %acts.1, bf16[1280,6400]{1,0:T(8,128)(2,1)} %w.1, bf16[64,1280]{1,0:T(8,128)(2,1)} %bitcast.27, bf16[64,6400]{1,0:T(8,128)(2,1)} %bitcast.26, bf16[64,6400]{1,0:T(8,128)(2,1)} %readout.1, ...), custom_call_target="tpu_custom_call" | custom-call | tf_op jit(solution)/shard_map/pallas_call | solution.py:778
  65.1 0.0 copy-start
  65.1 0.0 copy-start.1
  65.1 0.0 copy-done.3
  65.1 0.0 copy-done.4
  65.2 0.0 copy-done.5
  65.2 1.3 %subtract_convert_fusion.1 = (bf16[1,1280,64]{1,2,0:T(8,128)(2,1)}, f32[1,1280,64]{1,2,0:T(8,128)}, f32[1,1280,64]{1,2,0:T(8,128)}) fusion(bf16[1,1280,64]{1,2,0:T(8,128)(2,1)S(1)} %copy-done.3, f32[1,1280,64]{1,2,0:T(8,128)S(1)} %copy-done.4, f32[1,1280,64]{1,2,0:T(8,128)S(1)} %copy-done.5, bf16[256,1280]{1,0:T(8,128)(2,1)S(1)} %get-tuple-element.9, ...), kind=kOutput, calls=%fused_computation.11 | convolution fusion | flops 43171840 | bytes 2326528 | tf_op jit(solution)/shard_map/rd,rk->dk/dot_general | solution.py:846
  66.5 0.0 copy-done.2
  66.5 0.0 copy-done
  66.5 0.6 copy-done.1
  67.1 2.7 %subtract_convert_fusion = (bf16[1,64,6400]{2,1,0:T(8,128)(2,1)}, f32[1,64,6400]{2,1,0:T(8,128)}, f32[1,64,6400]{2,1,0:T(8,128)}) fusion(bf16[1,64,6400]{2,1,0:T(8,128)(2,1)S(1)} %copy-done, bf16[64,6400]{1,0:T(8,128)(2,1)S(1)} %get-tuple-element.11, f32[1,64,6400]{2,1,0:T(8,128)S(1)} %copy-done.1, f32[1,64,6400]{2,1,0:T(8,128)S(1)} %copy-done.2), kind=kLoop, calls=%fused_computation.6 | loop fusion | flops 6553600 | bytes 9011200 | tf_op jit(solution)/shard_map/convert_element_type | solution.py:29
Async XLA Ops:
  0.6 64.5 %copy-start.3 = (bf16[1,1280,64]{1,2,0:T(8,128)(2,1)S(1)}, bf16[1,1280,64]{1,2,0:T(8,128)(2,1)}, u32[]{:S(2)}) copy-start(bf16[1,1280,64]{1,2,0:T(8,128)(2,1)} %param.13) | copy-start | bytes 491524
  0.6 64.5 %copy-start.4 = (f32[1,1280,64]{1,2,0:T(8,128)S(1)}, f32[1,1280,64]{1,2,0:T(8,128)}, u32[]{:S(2)}) copy-start(f32[1,1280,64]{1,2,0:T(8,128)} %param.15) | copy-start | bytes 983044
  0.7 64.5 %copy-start.5 = (f32[1,1280,64]{1,2,0:T(8,128)S(1)}, f32[1,1280,64]{1,2,0:T(8,128)}, u32[]{:S(2)}) copy-start(f32[1,1280,64]{1,2,0:T(8,128)} %param.16) | copy-start | bytes 983044
  0.7 65.8 %copy-start.2 = (f32[1,64,6400]{2,1,0:T(8,128)S(1)}, f32[1,64,6400]{2,1,0:T(8,128)}, u32[]{:S(2)}) copy-start(f32[1,64,6400]{2,1,0:T(8,128)} %param.18) | copy-start | bytes 4915204
  65.1 1.4 %copy-start = (bf16[1,64,6400]{2,1,0:T(8,128)(2,1)S(1)}, bf16[1,64,6400]{2,1,0:T(8,128)(2,1)}, u32[]{:S(2)}) copy-start(bf16[1,64,6400]{2,1,0:T(8,128)(2,1)} %param.14) | copy-start | bytes 2457604
  65.1 2.0 %copy-start.1 = (f32[1,64,6400]{2,1,0:T(8,128)S(1)}, f32[1,64,6400]{2,1,0:T(8,128)}, u32[]{:S(2)}) copy-start(f32[1,64,6400]{2,1,0:T(8,128)} %param.17) | copy-start | bytes 4915204
